TPU v7x, 512 devices: a whole 4x4x16 slice. The times are simulated.
512 devices in a mesh: sub: 32 (over x_lo, z), beam: 16 (over x_hi, y, core).
Axes of the slice: x: 4 (x_hi: 2, x_lo: 2; x = x_hi * 2 + x_lo), y: 4, z: 16, core: 2. Of those that a mesh axis runs over, the one named last changes fastest.
Arguments:
- echoes: bfloat16 [64, 32, 2, 16384], P('sub', 'beam'), may hold values from -6 to 6
- matched_filter: float32 [2, 16384], replicated, may hold values from -6 to 6
- steering: bfloat16 [2, 128, 32], P(None, 'beam'), may hold values from -1 to 1
- kernels: bfloat16 [4, 2, 2, 128, 128], replicated, may hold values from -0.375 to 0.375
- blend_gains: float32 [4, 2, 2, 2], replicated, may hold values from 0.3 to 1
- beam_taps: int32 [4, 2, 2, 128], P(None, None, None, 'beam'), may hold values from -1 to 0
Outputs:
- polar_image: bfloat16 [64, 128, 2, 16384], P('sub', 'beam')
Inputs may be any that keep to these rules, and one draw needn't show every extreme that they name: `beam_taps`: a parent row n reads child rows n + t and n + t + 1.
All inputs are finite; a program needn't handle non-finite values.
Results may differ from a plain program's by a relative error of at most 0.019.
Values may be sent and summed in bfloat16 or wider, within the bound.
No kernel may reach another device: no remote copies, remote signals or barrier semaphores. Data moves between devices by JAX's collectives and lax.ppermute only.
A program may use at most 64 MiB of HBM per device.

v0:
```python
import math
import jax
import jax.numpy as jnp
import numpy as np
from jax import lax
from jax.sharding import Mesh
from jax.sharding import PartitionSpec as P

FA = 128
LEVELS = 4
HIGH = lax.Precision.HIGH


def table_product(form, left, right):
    return jnp.einsum(form, left, right, precision=HIGH)


def dft_tables(order, sign, modulus):
    index = np.arange(order)
    phase = index[:, None] * index[None, :] % modulus
    angle = phase * (sign * 2.0 * math.pi / modulus)
    return (jnp.asarray(np.cos(angle), jnp.float32), jnp.asarray(np.sin(angle), jnp.float32))


def four_step(real_part, imag_part, sign):
    order = real_part.shape[-1]
    cos_small, sin_small = dft_tables(order, sign, order)
    cos_turn, sin_turn = dft_tables(order, sign, order * order)
    first_real = table_product("kn,qnm->qkm", cos_small, real_part) - table_product(
        "kn,qnm->qkm", sin_small, imag_part
    )
    first_imag = table_product("kn,qnm->qkm", cos_small, imag_part) + table_product(
        "kn,qnm->qkm", sin_small, real_part
    )
    turned_real = first_real * cos_turn - first_imag * sin_turn
    turned_imag = first_real * sin_turn + first_imag * cos_turn
    out_real = table_product("qkm,mj->qjk", turned_real, cos_small) - table_product(
        "qkm,mj->qjk", turned_imag, sin_small
    )
    out_imag = table_product("qkm,mj->qjk", turned_real, sin_small) + table_product(
        "qkm,mj->qjk", turned_imag, cos_small
    )
    return (out_real, out_imag)


def compress(echoes, matched_filter):
    count = echoes.shape[0] * echoes.shape[1]
    length = echoes.shape[-1]
    signal = echoes.astype(jnp.float32).reshape(count, 2, FA, FA)
    spec_real, spec_imag = four_step(signal[:, 0], signal[:, 1], -1.0)
    matched = matched_filter.reshape(2, FA, FA)
    prod_real = spec_real * matched[0] - spec_imag * matched[1]
    prod_imag = spec_real * matched[1] + spec_imag * matched[0]
    back_real, back_imag = four_step(prod_real, prod_imag, 1.0)
    stacked = jnp.stack([back_real, back_imag], axis=1) / length
    return stacked.reshape(echoes.shape[:3] + (FA, FA)).astype(jnp.bfloat16)


def as_blocks(pair):
    real_part, imag_part = (pair[..., 0, :, :], pair[..., 1, :, :])
    top = jnp.concatenate([real_part, imag_part], axis=-1)
    bottom = jnp.concatenate([-imag_part, real_part], axis=-1)
    return jnp.concatenate([top, bottom], axis=-2)


def pick(table, index):
    return lax.dynamic_index_in_dim(table, index, 0, keepdims=False)


def range_chain(kernels, bits):
    blocks = as_blocks(kernels.astype(jnp.float32))
    chain = pick(blocks[3], bits[2])
    chain = table_product("ik,kj->ij", pick(blocks[2], bits[1]), chain)
    chain = table_product("ik,kj->ij", pick(blocks[1], bits[0]), chain)
    return table_product("cik,kj->cij", blocks[0], chain).astype(jnp.bfloat16)


def band_matrices(taps, gains):
    rows = taps.shape[0]
    first = jnp.moveaxis(taps, 0, -1).astype(jnp.int32)[..., None] + jnp.arange(rows)[:, None]
    column = jnp.arange(rows)
    lower = jnp.where(column == first, gains[..., 0, None, None], 0.0)
    upper = jnp.where(column == first + 1, gains[..., 1, None, None], 0.0)
    return lower + upper


def local(echoes, matched_filter, steering, kernels, blend_gains, beam_taps):
    zh = lax.axis_index("zh")
    zl = lax.axis_index("zl")
    own_rows = steering.shape[1]
    pulses = steering.shape[2]
    own_pulses = echoes.shape[1]
    beams = pulses // own_pulses
    packed = jnp.concatenate(
        [
            jnp.moveaxis(steering, 1, 0).reshape(own_rows, 2 * pulses),
            jnp.moveaxis(beam_taps, 3, 0).reshape(own_rows, 4 * LEVELS).astype(jnp.bfloat16),
        ],
        axis=1,
    )
    packed = jnp.pad(packed, ((0, 0), (0, 128 - packed.shape[1])))
    packed = lax.all_gather(packed, "beam", axis=0, tiled=True)
    rows = packed.shape[0]
    compressed = compress(echoes, matched_filter)
    mats = range_chain(kernels, (zl & 1, zl >> 1, zh)).reshape(2, 2, FA, 2, FA)
    turned = jnp.einsum(
        "spinm,simoj->sponj", compressed, mats, preferred_element_type=jnp.float32
    ).astype(jnp.bfloat16)
    width = 2 * own_pulses * 2
    peers = 4 * beams
    message = jnp.moveaxis(turned.reshape(width, peers, -1), 1, 0)
    own = lax.all_to_all(message, ("zl", "beam"), 0, 0, tiled=True).reshape(peers * width, -1)
    other = lax.ppermute(own, "zh", [(0, 1), (1, 0)])
    steer = packed[:, : 2 * pulses].astype(jnp.float32).reshape(rows, 2, beams, own_pulses)
    taps = packed[:, 2 * pulses : 2 * pulses + 4 * LEVELS].reshape(rows, LEVELS, 2, 2)
    band = band_matrices(taps, blend_gains)
    mixing = jnp.stack(
        [jnp.stack([steer[:, 0], -steer[:, 1]], -1), jnp.stack([steer[:, 1], steer[:, 0]], -1)], 1
    )
    lead = table_product("cenm,mobpi->enobcpi", band[0], mixing).reshape(2, rows, -1)
    lead = table_product("cenm,fmx->cefnx", band[1], lead)
    lead = table_product("cenm,dfgmx->cdefgnx", band[2], lead)

    def last(child):
        b4 = pick(pick(band[3], child), zh)
        full = table_product("nm,cdefgmx->cdefgnx", b4, lead).astype(jnp.bfloat16)
        full = full.reshape(2, 2, 2, 2, 2, beams, own_rows, 2, FA)
        full = jnp.transpose(full, (2, 3, 5, 4, 7, 6, 0, 1, 8))
        return full.reshape(4 * beams * 2 * 2 * own_rows, 4 * FA)

    total = jnp.dot(last(zh), own, preferred_element_type=jnp.float32)
    total = total + jnp.dot(last(1 - zh), other, preferred_element_type=jnp.float32)
    result = total.astype(jnp.bfloat16).reshape(peers, 2 * 2 * own_rows, -1)
    arrived = lax.all_to_all(result, ("zl", "beam"), 0, 0, tiled=True)
    arrived = arrived.reshape(peers, 2, 2, own_rows, -1)
    return jnp.transpose(arrived, (1, 3, 2, 0, 4)).reshape(2, own_rows, 2, -1)


def solution(mesh):
    fine = Mesh(mesh.devices.reshape(4, 2, 4, 16), ("g", "zh", "zl", "beam"))
    sub = ("g", "zh", "zl")
    return jax.shard_map(
        local,
        mesh=fine,
        in_specs=(
            P(sub, "beam", None, None),
            P(),
            P(None, "beam", None),
            P(),
            P(),
            P(None, None, None, "beam"),
        ),
        out_specs=P(sub, "beam", None, None),
        check_vma=False,
    )
```

profile of v0, /device:TPU:1, one launch (start us, length us, event | category | flops | bytes accessed | tf_op | source)
XLA Modules:
  0.0 150.1 jit_solution(6426579035786599615)
XLA Ops:
  0.0 1.2 reshape.128
  1.2 1.1 fusion.34
  2.3 1.1 fusion.33
  3.4 1.1 convolution_add_fusion.4
  4.4 0.2 convolution_subtract_fusion.3
  4.7 0.3 fusion.20
  5.0 0.3 fusion.22
  5.2 0.3 fusion.13
  5.5 0.3 fusion.14
  6.1 0.3 fusion.43
  6.4 0.3 fusion.44
  6.7 0.3 fusion.12
  7.0 0.3 fusion.11
  7.3 0.4 fusion.36
  7.7 0.4 fusion.35
  8.2 0.9 slice_bitcast_fusion.2
  9.2 0.4 convolution_subtract_fusion
  9.7 0.4 convolution_add_fusion.1
  10.1 0.8 copy.172
  10.9 1.4 maximum_maximum_fusion
  12.3 1.0 fusion.59
  13.3 0.3 fusion.25
  13.6 1.3 convolution_bitcast_fusion.3
  14.8 0.4 convolution_convert_fusion
  15.3 0.3 fusion.10
  15.6 0.2 copy.174
  15.9 0.9 copy.175
  16.8 13.1 %all-to-all-start = ((bf16[64,8,256]{2,1,0:T(8,128)(2,1)}), bf16[64,8,256]{2,1,0:T(8,128)(2,1)S(1)}, u32[]{:S(2)}, u32[]{:S(2)}) async-start(bf16[64,8,256]{2,1,0:T(8,128)(2,1)} %copy.175), calls=%async_computation | async-start | bytes 524288 | tf_op jit(solution)/shard_map/all_to_all | solution.py:112
  30.1 24.7 %all_gather.3 = bf16[128,128]{1,0:T(8,128)(2,1)S(1)} all-gather(bf16[8,128]{1,0:T(8,128)(2,1)S(1)} %fusion.47), channel_id=1, replica_groups=mesh['g'=4,'zh'=2,'zl'=4,'beam'=16] {'beam'}, dimensions={0}, use_global_device_ids=true | all-gather | bytes 34816 | tf_op jit(solution)/shard_map/all_gather | solution.py:102
  55.3 0.6 select_add_fusion
  56.0 0.3 convolution_bitcast_fusion.4
  56.3 0.2 copy.158
  56.5 0.6 convolution_bitcast_fusion.1
  57.1 1.9 %convolution_bitcast_fusion = f32[2,2,2,2,2,128,256]{5,6,2,0,4,3,1:T(8,128)S(1)} fusion(f32[2,2,2,128,256,1,1]{3,4,6,5,2,1,0:T(8,128)S(1)} %convolution_bitcast_fusion.1, f32[4,2,2,128,128]{4,3,2,1,0:T(8,128)S(1)} %select_add_fusion), kind=kOutput, calls=%fused_computation.6 | convolution fusion | flops 805306368 | bytes 5505024 | tf_op jit(solution)/shard_map/cenm,dfgmx->cdefgnx/dot_general | solution.py:15
  59.0 1.9 %copy-done = f32[2,2,2,2,2,128,256]{5,6,2,0,4,3,1:T(8,128)} copy-done((f32[2,2,2,2,2,128,256]{5,6,2,0,4,3,1:T(8,128)}, f32[2,2,2,2,2,128,256]{5,6,2,0,4,3,1:T(8,128)S(1)}, u32[]{:S(2)}) %copy-start) | copy-done | bytes 4194328
  60.9 2.0 %convert_bitcast_fusion.1 = bf16[2,2,2,2,2,128,256]{5,6,4,3,2,1,0:T(8,128)(2,1)S(1)} fusion(f32[2,2,2,2,2,128,256]{5,6,2,0,4,3,1:T(8,128)S(1)} %convolution_bitcast_fusion, f32[1,2,2,128,128]{4,3,2,1,0:T(8,128)S(1)} %slice.94, s32[]{:T(128)S(6)} %select_n.32), kind=kOutput, calls=%fused_computation.9 | convolution fusion | flops 806354944 | bytes 6356996 | tf_op jit(solution)/shard_map/nm,cdefgmx->cdefgnx/dot_general | solution.py:15
  63.0 2.4 %copy.160 = bf16[2,2,2,2,2,128,256]{6,5,4,3,2,1,0:T(8,128)(2,1)} copy(bf16[2,2,2,2,2,128,256]{5,6,4,3,2,1,0:T(8,128)(2,1)S(1)} %convert_bitcast_fusion.1) | data formatting | bytes 4194304 | tf_op jit(solution)/shard_map/convert_element_type | solution.py:126
  65.3 2.2 %copy.161 = bf16[2,2,16,2,2,8,2,2,128]{8,5,7,6,4,3,2,1,0:T(8,128)(2,1)S(1)} copy(bf16[2,2,16,2,2,8,2,2,128]{8,5,4,2,3,1,0,7,6:T(8,128)(2,1)} %bitcast.206) | data formatting | bytes 4194304 | tf_op jit(solution)/shard_map/transpose | solution.py:128
  67.5 5.4 %convert_bitcast_fusion = bf16[2,2,2,2,2,128,256]{5,6,4,3,2,1,0:T(8,128)(2,1)} fusion(f32[2,2,2,2,2,128,256]{5,6,2,0,4,3,1:T(8,128)} %copy-done, f32[1,2,2,128,128]{4,3,2,1,0:T(8,128)S(1)} %slice.94, s32[]{:T(128)S(6)} %select_n.36, s32[]{:T(128)S(6)} %select_n.32), kind=kOutput, calls=%fused_computation.8 | convolution fusion | flops 806354944 | bytes 6357000 | tf_op jit(solution)/shard_map/nm,cdefgmx->cdefgnx/dot_general | solution.py:15
  72.9 4.1 %copy.177 = bf16[2,2,2,2,2,128,256]{6,5,4,3,2,1,0:T(8,128)(2,1)} copy(bf16[2,2,2,2,2,128,256]{5,6,4,3,2,1,0:T(8,128)(2,1)} %convert_bitcast_fusion) | data formatting | bytes 4194304 | tf_op jit(solution)/shard_map/convert_element_type | solution.py:126
  77.0 3.5 %copy.178 = bf16[2,2,16,2,2,8,2,2,128]{8,5,7,6,4,3,2,1,0:T(8,128)(2,1)} copy(bf16[2,2,16,2,2,8,2,2,128]{8,5,4,2,3,1,0,7,6:T(8,128)(2,1)} %bitcast.207) | data formatting | bytes 4194304 | tf_op jit(solution)/shard_map/transpose | solution.py:128
  80.5 8.8 %collective-permute-start = (bf16[512,256]{1,0:T(8,128)(2,1)S(1)}, bf16[512,256]{1,0:T(8,128)(2,1)S(1)}, u32[]{:S(2)}, u32[]{:S(2)}) collective-permute-start(bf16[512,256]{1,0:T(8,128)(2,1)S(1)} %bitcast.216), channel_id=1, source_target_pairs={{0,64},{64,0},{1,65},{65,1},{2,66},{66,2},{3,67},{67,3},{4,68},{68... | collective-permute-start | bytes 786440 | tf_op jit(solution)/shard_map/ppermute | solution.py:113
  89.3 0.7 fusion.54
  90.0 22.7 %collective-permute-done = bf16[512,256]{1,0:T(8,128)(2,1)S(1)} collective-permute-done((bf16[512,256]{1,0:T(8,128)(2,1)S(1)}, bf16[512,256]{1,0:T(8,128)(2,1)S(1)}, u32[]{:S(2)}, u32[]{:S(2)}) %collective-permute-start) | collective-permute-done | bytes 262176 | tf_op jit(solution)/shard_map/ppermute | solution.py:113
  112.8 0.7 fusion.4
  113.5 34.9 %all_to_all.10 = bf16[64,32,256]{2,1,0:T(8,128)(2,1)S(1)} all-to-all(bf16[64,32,256]{2,1,0:T(8,128)(2,1)S(1)} %bitcast.210), channel_id=1, replica_groups=mesh['g'=4,'zh'=2,'zl'=4,'beam'=16] {'zl','beam'}, dimensions={0} | all-to-all | bytes 2097152 | tf_op jit(solution)/shard_map/all_to_all | solution.py:134
  148.4 0.6 copy.221
  149.0 1.1 reshape.109
  (55 shorter events, 1.5 us)
Async XLA Ops:
  0.0 5.0 %copy-start.2 = (f32[128,128,1]{1,0,2:T(8,128)S(1)}, f32[128,128,1]{1,0,2:T(8,128)}, u32[]{:S(2)}) copy-start(f32[128,128,1]{1,0,2:T(8,128)} %constant.123) | copy-start | bytes 196612
  0.0 4.4 %copy-start.7 = (f32[128,128,1]{1,0,2:T(8,128)S(1)}, f32[128,128,1]{1,0,2:T(8,128)}, u32[]{:S(2)}) copy-start(f32[128,128,1]{1,0,2:T(8,128)} %constant.124) | copy-start | bytes 196612
  0.0 4.6 %copy-start.8 = (f32[128,128]{1,0:T(8,128)S(1)}, f32[128,128]{1,0:T(8,128)}, u32[]{:S(2)}) copy-start(f32[128,128]{1,0:T(8,128)} %constant.114.clone) | copy-start | bytes 196612
  0.0 4.7 %copy-start.9 = (f32[128,128]{1,0:T(8,128)S(1)}, f32[128,128]{1,0:T(8,128)}, u32[]{:S(2)}) copy-start(f32[128,128]{1,0:T(8,128)} %constant.115.clone) | copy-start | bytes 196612
  4.7 1.1 copy-start.11
  5.5 1.2 copy-start.4
  6.1 1.2 copy-start.5
  6.1 1.2 copy-start.6
  6.7 1.4 copy-start.10
  13.5 1.8 %copy-start.3 = (f32[2,2,1,128,128]{4,3,2,1,0:T(8,128)S(1)}, f32[2,2,1,128,128]{4,3,2,1,0:T(8,128)}, u32[]{:S(2)}) copy-start(f32[2,2,1,128,128]{4,3,2,1,0:T(8,128)} %copy.172) | copy-start | bytes 786436
  15.2 14.6 %copy-start.12 = (s32[4,2,2,8]{3,2,1,0:T(2,128)S(1)}, s32[4,2,2,8]{3,2,1,0:T(2,128)}, u32[]{:S(2)}) copy-start(s32[4,2,2,8]{3,2,1,0:T(2,128)} %param.19) | copy-start | bytes 1540
  15.2 14.7 %copy-start.13 = (bf16[2,8,32]{2,1,0:T(8,128)(2,1)S(1)}, bf16[2,8,32]{2,1,0:T(8,128)(2,1)}, u32[]{:S(2)}) copy-start(bf16[2,8,32]{2,1,0:T(8,128)(2,1)} %param.16) | copy-start | bytes 3076
  15.2 39.9 %copy-start.14 = (f32[4,2,2,2]{0,3,2,1:T(2,128)S(1)}, f32[4,2,2,2]{0,3,2,1:T(2,128)}, u32[]{:S(2)}) copy-start(f32[4,2,2,2]{0,3,2,1:T(2,128)} %param.18) | copy-start | bytes 388
  16.8 63.7 %all-to-all-start = ((bf16[64,8,256]{2,1,0:T(8,128)(2,1)}), bf16[64,8,256]{2,1,0:T(8,128)(2,1)S(1)}, u32[]{:S(2)}, u32[]{:S(2)}) async-start(bf16[64,8,256]{2,1,0:T(8,128)(2,1)} %copy.175), calls=%async_computation | async-start | bytes 524288 | tf_op jit(solution)/shard_map/all_to_all | solution.py:112
  59.0 1.9 %copy-start = (f32[2,2,2,2,2,128,256]{5,6,2,0,4,3,1:T(8,128)}, f32[2,2,2,2,2,128,256]{5,6,2,0,4,3,1:T(8,128)S(1)}, u32[]{:S(2)}) copy-start(f32[2,2,2,2,2,128,256]{5,6,2,0,4,3,1:T(8,128)S(1)} %convolution_bitcast_fusion) | copy-start | bytes 12582916
  80.5 32.3 %collective-permute-start = (bf16[512,256]{1,0:T(8,128)(2,1)S(1)}, bf16[512,256]{1,0:T(8,128)(2,1)S(1)}, u32[]{:S(2)}, u32[]{:S(2)}) collective-permute-start(bf16[512,256]{1,0:T(8,128)(2,1)S(1)} %bitcast.216), channel_id=1, source_target_pairs={{0,64},{64,0},{1,65},{65,1},{2,66},{66,2},{3,67},{67,3},{4,68},{68... | collective-permute-start | bytes 786440 | tf_op jit(solution)/shard_map/ppermute | solution.py:113
  89.3 23.4 %copy-start.1 = (bf16[2,2,16,2,2,8,2,2,128]{8,5,7,6,4,3,2,1,0:T(8,128)(2,1)S(1)}, bf16[2,2,16,2,2,8,2,2,128]{8,5,7,6,4,3,2,1,0:T(8,128)(2,1)}, u32[]{:S(2)}) copy-start(bf16[2,2,16,2,2,8,2,2,128]{8,5,7,6,4,3,2,1,0:T(8,128)(2,1)} %copy.178) | copy-start | bytes 6291460
where the time goes:
time: 151 us; the launch traced here: 150 us
  blocking collectives  59.6 us (39%)
  waiting for transfers between devices  22.7 us (15%)
  local copies, waits for them, and re-layouts  22.1 us (15%)
  starting transfers between devices  21.9 us (15%)
  matrix products  20.8 us (14%)
  other arithmetic  2.36 us (2%)
    all_to_all x1, blocking collectives, local(): arrived = lax.all_to_all(result, ('zl', 'beam'), 0, 0, tiled=True)  34.9 us
    all_gather x1, blocking collectives, local(): packed = lax.all_gather(packed, 'beam', axis=0, tiled=True)  24.7 us
    ppermute x1, waiting for transfers between devices, local(): other = lax.ppermute(own, 'zh', [(0, 1), (1, 0)])  22.7 us
    dot_general x24, matrix products, table_product(): return jnp.einsum(form, left, right, precision=HIGH)  19.1 us
    all_to_all x1, starting transfers between devices, local(): lax.all_to_all(message, ('zl', 'beam'), 0, 0, tiled=True)  13.1 us
    ppermute x1, starting transfers between devices, local(): other = lax.ppermute(own, 'zh', [(0, 1), (1, 0)])  8.81 us
    convert_element_type x2, local copies, waits for them, and re-layouts, last(): full = table_product('nm,cdefgmx->cdefgnx', b4, lead).astype(jnp.bfloat16)  6.51 us
    transpose x2, local copies, waits for them, and re-layouts, last(): full = jnp.transpose(full, (2, 3, 5, 4, 7, 6, 0, 1, 8))  5.65 us
  transfers between devices with their start and end apart: 2, of which 1 were waited for; matrix products, arithmetic and copies ran while one was open for 16% of the time, Pallas kernels for 0%

commit v1 on v0

--- a/solution.py
+++ b/solution.py
@@ -99,7 +99,12 @@
         axis=1,
     )
     packed = jnp.pad(packed, ((0, 0), (0, 128 - packed.shape[1])))
-    packed = lax.all_gather(packed, "beam", axis=0, tiled=True)
+    packed = jnp.concatenate(
+        lax.all_to_all(
+            jnp.stack(tuple((packed for _ in range(lax.axis_size("beam"))))), "beam", 0, 0
+        ),
+        axis=0,
+    )
     rows = packed.shape[0]
     compressed = compress(echoes, matched_filter)
     mats = range_chain(kernels, (zl & 1, zl >> 1, zh)).reshape(2, 2, FA, 2, FA)

time: 151 us -> 139 us (0.921)
  blocking collectives: 59.6 us -> 40.4 us
  starting transfers between devices: 21.9 us -> 29.1 us
  matrix products: 20.8 us -> 18.5 us
  local copies, waits for them, and re-layouts: 22.1 us -> 24 us
    all_gather x1 -> x0, blocking collectives: 24.7 us -> none  [local(): packed = lax.all_gather(packed, 'beam', axis=0, tiled=True)]
    all_to_all x0 -> x1, starting transfers between devices: none -> 10.1 us  [local(): lax.all_to_all(jnp.stack(tuple((packed for _ in range(lax.axis_size('beam...]
    all_to_all x1, blocking collectives: 34.9 us -> 40.4 us  [local(): arrived = lax.all_to_all(result, ('zl', 'beam'), 0, 0, tiled=True)]
    all_to_all x1, starting transfers between devices: 13.1 us -> 10.2 us  [local(): lax.all_to_all(message, ('zl', 'beam'), 0, 0, tiled=True)]
    dot_general x24, matrix products: 19.1 us -> 16.8 us  [table_product(): return jnp.einsum(form, left, right, precision=HIGH)]
  transfers between devices with their start and end apart: 2 -> 3, of which waited for: 1 -> 1; matrix products, arithmetic and copies ran while one was open for 16% -> 28% of each run, Pallas kernels for 0% -> 0%
where the time goes in v1:
time: 139 us; the launch traced here: 138 us
  blocking collectives  40.4 us (29%)
  starting transfers between devices  29.1 us (21%)
  local copies, waits for them, and re-layouts  24 us (17%)
  waiting for transfers between devices  22.2 us (16%)
  matrix products  18.5 us (13%)
  other arithmetic  3.09 us (2%)
    all_to_all x1, blocking collectives, local(): arrived = lax.all_to_all(result, ('zl', 'beam'), 0, 0, tiled=True)  40.4 us
    ppermute x1, waiting for transfers between devices, local(): other = lax.ppermute(own, 'zh', [(0, 1), (1, 0)])  22.2 us
    dot_general x24, matrix products, table_product(): return jnp.einsum(form, left, right, precision=HIGH)  16.8 us
    all_to_all x1, starting transfers between devices, local(): lax.all_to_all(message, ('zl', 'beam'), 0, 0, tiled=True)  10.2 us
    all_to_all x1, starting transfers between devices, local(): lax.all_to_all(jnp.stack(tuple((packed for _ in range(lax.axis_size('beam...  10.1 us
    ppermute x1, starting transfers between devices, local(): other = lax.ppermute(own, 'zh', [(0, 1), (1, 0)])  8.79 us
    convert_element_type x2, local copies, waits for them, and re-layouts, last(): full = table_product('nm,cdefgmx->cdefgnx', b4, lead).astype(jnp.bfloat16)  6.5 us
    transpose x2, local copies, waits for them, and re-layouts, last(): full = jnp.transpose(full, (2, 3, 5, 4, 7, 6, 0, 1, 8))  5.8 us
  transfers between devices with their start and end apart: 3, of which 1 were waited for; matrix products, arithmetic and copies ran while one was open for 28% of the time, Pallas kernels for 0%

profile of v1, /device:TPU:1, one launch (start us, length us, event | category | flops | bytes accessed | tf_op | source)
XLA Modules:
  0.0 137.9 jit_solution(13612512444076500274)
XLA Ops:
  0.0 0.7 convert_element_type.52
  0.9 0.7 copy.122
  1.7 0.6 stack.18
  2.3 10.1 %all-to-all-start = ((bf16[16,8,128]{2,1,0:T(8,128)(2,1)}), bf16[16,8,128]{2,1,0:T(8,128)(2,1)S(1)}, u32[]{:S(2)}, u32[]{:S(2)}) async-start(bf16[16,8,128]{2,1,0:T(8,128)(2,1)} %stack.18), calls=%async_computation | async-start | bytes 65536 | tf_op jit(solution)/shard_map/all_to_all | solution.py:103
  12.5 1.2 reshape.134
  13.6 1.1 fusion.34
  14.7 1.1 fusion.33
  15.7 1.1 convolution_add_fusion.4
  17.1 0.3 fusion.20
  17.6 0.3 fusion.13
  17.9 0.3 fusion.14
  18.5 0.3 fusion.43
  18.8 0.3 fusion.44
  19.1 0.3 fusion.12
  19.4 0.3 fusion.11
  19.7 0.4 fusion.36
  20.1 0.4 fusion.35
  20.6 0.9 slice_bitcast_fusion.2
  21.5 0.4 convolution_subtract_fusion
  22.1 0.4 convolution_add_fusion.1
  22.5 0.8 copy.144
  23.3 1.4 %maximum_maximum_fusion = f32[4,2,256,256]{3,2,1,0:T(8,128)S(1)} fusion(f32[4,2,128,128]{3,2,1,0:T(8,128)} %get-tuple-element.9, f32[4,2,128,128]{3,2,1,0:T(8,128)S(1)} %fusion.58, f32[4,2,128,128]{3,2,1,0:T(8,128)S(1)} %get-tuple-element.8), kind=kLoop, calls=%fused_computation.7 | loop fusion | flops 1572864 | bytes 3670016 | tf_op jit(solution)/shard_map/concatenate | solution.py:63
  24.7 1.0 fusion.59
  25.7 0.3 fusion.25
  25.9 1.3 convolution_bitcast_fusion.3
  27.2 0.4 convolution_convert_fusion
  27.7 0.3 fusion.10
  28.3 0.9 copy.147
  29.3 10.2 %all-to-all-start.1 = ((bf16[64,8,256]{2,1,0:T(8,128)(2,1)}), bf16[64,8,256]{2,1,0:T(8,128)(2,1)S(1)}, u32[]{:S(2)}, u32[]{:S(2)}) async-start(bf16[64,8,256]{2,1,0:T(8,128)(2,1)} %copy.147), calls=%async_computation.1 | async-start | bytes 524288 | tf_op jit(solution)/shard_map/all_to_all | solution.py:117
  39.8 0.6 select_add_fusion
  40.5 0.3 convolution_bitcast_fusion.4
  41.0 0.6 convolution_bitcast_fusion.1
  41.6 1.9 %convolution_bitcast_fusion = f32[2,2,2,2,2,128,256]{5,6,2,0,4,3,1:T(8,128)S(1)} fusion(f32[2,2,2,128,256,1,1]{3,4,6,5,2,1,0:T(8,128)S(1)} %convolution_bitcast_fusion.1, f32[4,2,2,128,128]{4,3,2,1,0:T(8,128)S(1)} %select_add_fusion), kind=kOutput, calls=%fused_computation.6 | convolution fusion | flops 805306368 | bytes 5505024 | tf_op jit(solution)/shard_map/cenm,dfgmx->cdefgnx/dot_general | solution.py:15
  43.5 1.9 %copy-done = f32[2,2,2,2,2,128,256]{5,6,2,0,4,3,1:T(8,128)} copy-done((f32[2,2,2,2,2,128,256]{5,6,2,0,4,3,1:T(8,128)}, f32[2,2,2,2,2,128,256]{5,6,2,0,4,3,1:T(8,128)S(1)}, u32[]{:S(2)}) %copy-start) | copy-done | bytes 4194328
  45.4 2.0 %convert_bitcast_fusion.1 = bf16[2,2,2,2,2,128,256]{5,6,4,3,2,1,0:T(8,128)(2,1)S(1)} fusion(f32[2,2,2,2,2,128,256]{5,6,2,0,4,3,1:T(8,128)S(1)} %convolution_bitcast_fusion, f32[1,2,2,128,128]{4,3,2,1,0:T(8,128)S(1)} %slice.94, s32[]{:T(128)S(6)} %select_n.32), kind=kOutput, calls=%fused_computation.9 | convolution fusion | flops 806354944 | bytes 6356996 | tf_op jit(solution)/shard_map/nm,cdefgmx->cdefgnx/dot_general | solution.py:15
  47.4 2.4 %copy.132 = bf16[2,2,2,2,2,128,256]{6,5,4,3,2,1,0:T(8,128)(2,1)} copy(bf16[2,2,2,2,2,128,256]{5,6,4,3,2,1,0:T(8,128)(2,1)S(1)} %convert_bitcast_fusion.1) | data formatting | bytes 4194304 | tf_op jit(solution)/shard_map/convert_element_type | solution.py:131
  49.8 2.3 %copy.133 = bf16[2,2,16,2,2,8,2,2,128]{8,5,7,6,4,3,2,1,0:T(8,128)(2,1)S(1)} copy(bf16[2,2,16,2,2,8,2,2,128]{8,5,4,2,3,1,0,7,6:T(8,128)(2,1)} %bitcast.207) | data formatting | bytes 4194304 | tf_op jit(solution)/shard_map/transpose | solution.py:133
  52.1 0.5 copy-done.1
  52.6 3.1 %convert_bitcast_fusion = bf16[2,2,2,2,2,128,256]{5,6,4,3,2,1,0:T(8,128)(2,1)} fusion(f32[2,2,2,2,2,128,256]{5,6,2,0,4,3,1:T(8,128)S(1)} %copy-done.1, f32[1,2,2,128,128]{4,3,2,1,0:T(8,128)S(1)} %slice.94, s32[]{:T(128)S(6)} %select_n.36, s32[]{:T(128)S(6)} %select_n.32), kind=kOutput, calls=%fused_computation.8 | convolution fusion | flops 806354944 | bytes 6357000 | tf_op jit(solution)/shard_map/nm,cdefgmx->cdefgnx/dot_general | solution.py:15
  55.7 4.1 %copy.149 = bf16[2,2,2,2,2,128,256]{6,5,4,3,2,1,0:T(8,128)(2,1)} copy(bf16[2,2,2,2,2,128,256]{5,6,4,3,2,1,0:T(8,128)(2,1)} %convert_bitcast_fusion) | data formatting | bytes 4194304 | tf_op jit(solution)/shard_map/convert_element_type | solution.py:131
  59.8 3.5 %copy.150 = bf16[2,2,16,2,2,8,2,2,128]{8,5,7,6,4,3,2,1,0:T(8,128)(2,1)} copy(bf16[2,2,16,2,2,8,2,2,128]{8,5,4,2,3,1,0,7,6:T(8,128)(2,1)} %bitcast.208) | data formatting | bytes 4194304 | tf_op jit(solution)/shard_map/transpose | solution.py:133
  63.3 8.8 %collective-permute-start = (bf16[512,256]{1,0:T(8,128)(2,1)S(1)}, bf16[512,256]{1,0:T(8,128)(2,1)S(1)}, u32[]{:S(2)}, u32[]{:S(2)}) collective-permute-start(bf16[512,256]{1,0:T(8,128)(2,1)S(1)} %bitcast.217), channel_id=1, source_target_pairs={{0,64},{64,0},{1,65},{65,1},{2,66},{66,2},{3,67},{67,3},{4,68},{68... | collective-permute-start | bytes 786440 | tf_op jit(solution)/shard_map/ppermute | solution.py:118
  72.1 0.7 fusion.54
  72.8 22.2 %collective-permute-done = bf16[512,256]{1,0:T(8,128)(2,1)S(1)} collective-permute-done((bf16[512,256]{1,0:T(8,128)(2,1)S(1)}, bf16[512,256]{1,0:T(8,128)(2,1)S(1)}, u32[]{:S(2)}, u32[]{:S(2)}) %collective-permute-start) | collective-permute-done | bytes 262176 | tf_op jit(solution)/shard_map/ppermute | solution.py:118
  95.0 0.7 fusion.4
  95.7 40.4 %all_to_all.15 = bf16[64,32,256]{2,1,0:T(8,128)(2,1)S(1)} all-to-all(bf16[64,32,256]{2,1,0:T(8,128)(2,1)S(1)} %bitcast.211), channel_id=1, replica_groups=mesh['g'=4,'zh'=2,'zl'=4,'beam'=16] {'zl','beam'}, dimensions={0} | all-to-all | bytes 2097152 | tf_op jit(solution)/shard_map/all_to_all | solution.py:139
  136.2 0.6 copy.193
  136.8 1.1 reshape.115
  (55 shorter events, 2.4 us)
Async XLA Ops:
  0.0 17.3 %copy-start.3 = (f32[128,128,1]{1,0,2:T(8,128)S(1)}, f32[128,128,1]{1,0,2:T(8,128)}, u32[]{:S(2)}) copy-start(f32[128,128,1]{1,0,2:T(8,128)} %constant.123) | copy-start | bytes 196612
  0.0 16.8 %copy-start.8 = (f32[128,128,1]{1,0,2:T(8,128)S(1)}, f32[128,128,1]{1,0,2:T(8,128)}, u32[]{:S(2)}) copy-start(f32[128,128,1]{1,0,2:T(8,128)} %constant.124) | copy-start | bytes 196612
  0.0 17.0 %copy-start.9 = (f32[128,128]{1,0:T(8,128)S(1)}, f32[128,128]{1,0:T(8,128)}, u32[]{:S(2)}) copy-start(f32[128,128]{1,0:T(8,128)} %constant.114.clone) | copy-start | bytes 196612
  0.0 17.0 %copy-start.10 = (f32[128,128]{1,0:T(8,128)S(1)}, f32[128,128]{1,0:T(8,128)}, u32[]{:S(2)}) copy-start(f32[128,128]{1,0:T(8,128)} %constant.115.clone) | copy-start | bytes 196612
  2.3 27.0 %all-to-all-start = ((bf16[16,8,128]{2,1,0:T(8,128)(2,1)}), bf16[16,8,128]{2,1,0:T(8,128)(2,1)S(1)}, u32[]{:S(2)}, u32[]{:S(2)}) async-start(bf16[16,8,128]{2,1,0:T(8,128)(2,1)} %stack.18), calls=%async_computation | async-start | bytes 65536 | tf_op jit(solution)/shard_map/all_to_all | solution.py:103
  17.1 1.1 copy-start.12
  17.9 1.2 copy-start.5
  18.5 1.2 copy-start.6
  18.5 1.2 copy-start.7
  19.1 1.4 %copy-start.11 = (bf16[4,2,2,128,128]{4,3,2,1,0:T(8,128)(2,1)S(1)}, bf16[4,2,2,128,128]{4,3,2,1,0:T(8,128)(2,1)}, u32[]{:S(2)}) copy-start(bf16[4,2,2,128,128]{4,3,2,1,0:T(8,128)(2,1)} %param.17) | copy-start | bytes 1572868
  25.7 2.3 %copy-start.13 = (f32[4,2,2,2]{0,3,2,1:T(2,128)S(1)}, f32[4,2,2,2]{0,3,2,1:T(2,128)}, u32[]{:S(2)}) copy-start(f32[4,2,2,2]{0,3,2,1:T(2,128)} %param.18) | copy-start | bytes 388
  25.9 1.7 %copy-start.4 = (f32[2,2,1,128,128]{4,3,2,1,0:T(8,128)S(1)}, f32[2,2,1,128,128]{4,3,2,1,0:T(8,128)}, u32[]{:S(2)}) copy-start(f32[2,2,1,128,128]{4,3,2,1,0:T(8,128)} %copy.144) | copy-start | bytes 786436
  29.3 34.0 %all-to-all-start.1 = ((bf16[64,8,256]{2,1,0:T(8,128)(2,1)}), bf16[64,8,256]{2,1,0:T(8,128)(2,1)S(1)}, u32[]{:S(2)}, u32[]{:S(2)}) async-start(bf16[64,8,256]{2,1,0:T(8,128)(2,1)} %copy.147), calls=%async_computation.1 | async-start | bytes 524288 | tf_op jit(solution)/shard_map/all_to_all | solution.py:117
  43.5 1.9 %copy-start = (f32[2,2,2,2,2,128,256]{5,6,2,0,4,3,1:T(8,128)}, f32[2,2,2,2,2,128,256]{5,6,2,0,4,3,1:T(8,128)S(1)}, u32[]{:S(2)}) copy-start(f32[2,2,2,2,2,128,256]{5,6,2,0,4,3,1:T(8,128)S(1)} %convolution_bitcast_fusion) | copy-start | bytes 12582916
  49.8 2.8 %copy-start.1 = (f32[2,2,2,2,2,128,256]{5,6,2,0,4,3,1:T(8,128)S(1)}, f32[2,2,2,2,2,128,256]{5,6,2,0,4,3,1:T(8,128)}, u32[]{:S(2)}) copy-start(f32[2,2,2,2,2,128,256]{5,6,2,0,4,3,1:T(8,128)} %copy-done) | copy-start | bytes 12582916
  63.3 31.7 %collective-permute-start = (bf16[512,256]{1,0:T(8,128)(2,1)S(1)}, bf16[512,256]{1,0:T(8,128)(2,1)S(1)}, u32[]{:S(2)}, u32[]{:S(2)}) collective-permute-start(bf16[512,256]{1,0:T(8,128)(2,1)S(1)} %bitcast.217), channel_id=1, source_target_pairs={{0,64},{64,0},{1,65},{65,1},{2,66},{66,2},{3,67},{67,3},{4,68},{68... | collective-permute-start | bytes 786440 | tf_op jit(solution)/shard_map/ppermute | solution.py:118
  72.1 22.9 %copy-start.2 = (bf16[2,2,16,2,2,8,2,2,128]{8,5,7,6,4,3,2,1,0:T(8,128)(2,1)S(1)}, bf16[2,2,16,2,2,8,2,2,128]{8,5,7,6,4,3,2,1,0:T(8,128)(2,1)}, u32[]{:S(2)}) copy-start(bf16[2,2,16,2,2,8,2,2,128]{8,5,7,6,4,3,2,1,0:T(8,128)(2,1)} %copy.150) | copy-start | bytes 6291460
